TPU v7x, 32 devices: a whole 2x2x4 slice. The times are simulated.
32 devices in a mesh: member: 4 (over y, core), tile: 8 (over z, x).
Axes of the slice: x: 2, y: 2, z: 4, core: 2. Of those that a mesh axis runs over, the one named last changes fastest.
Arguments:
- perturb: bfloat16 [64, 128, 2560], P('member', 'tile'), may hold values from -0.75 to 0.75
- weights: float32 [64, 32, 1280], P('member', 'tile'), may hold values from -1.2 to 1.2
- column_map: bfloat16 [1280, 2560], replicated, may hold values from -0.15625 to 0.15625
- background: float32 [128, 2560], P('tile', 'member'), may hold values from -6 to 6
- stencil_index: int32 [8, 32, 4, 8], P('tile'), may hold values from 0 to 9598, as said below
- row_fraction: float32 [8, 32, 4, 8], P('tile'), may hold values from 0 to 1
- column_fraction: float32 [8, 32, 4, 8], P('tile'), may hold values from 0 to 1
- block_lengths: int32 [8, 32, 4], P('tile'), may hold values from 0 to 8, as said below
- obs_value: float32 [32, 32, 8], P(('member', 'tile')), may hold values from -6 to 6
- obs_error: float32 [32, 32, 8], P(('member', 'tile')), may hold values from 0.3 to 1
- instrument_gain: float32 [32], P(('member', 'tile')), may hold values from 0.2 to 0.8
Outputs:
- analysis_weights: float32 [64, 32, 1280], P('member', 'tile')
- analysis_increment: float32 [128, 2560], P('tile', 'member')
Inputs may be any that keep to these rules, and one draw needn't show every extreme that they name: stencil_index = r * 640 + c with 0 <= r < 15 and 0 <= c < 639. `block_lengths`: in every draw some owner (one tile and one member index) has all its blocks full.
All inputs are finite; a program needn't handle non-finite values.
Results may differ from a plain program's by a relative error of at most 0.0022.
Values may be sent and summed in bfloat16 or wider, within the bound.
A program may use at most 64 MiB of HBM per device.

v0:
```python
import jax
import jax.numpy as jnp
from jax import lax
from jax.sharding import PartitionSpec as P

RATIO = 4
KSM = 3


DIFFUSION = 0.45


def padded(block, sides, width):
    for axis, dim in sides:
        count = lax.axis_size(axis)
        forward = [(i, i + 1) for i in range(count - 1)]
        backward = [(target, source) for source, target in forward]
        low = lax.ppermute(
            lax.slice_in_dim(block, block.shape[dim] - width, None, axis=dim), axis, forward
        )
        high = lax.ppermute(lax.slice_in_dim(block, 0, width, axis=dim), axis, backward)
        block = jnp.concatenate([low, block, high], axis=dim)
    return block


def rows_halo(grid_values, width_rows):
    return padded(grid_values, (("tile", 1),), width_rows)


def smoothed(grid_values, extra_rows):
    rim_depth = KSM + extra_rows
    extended = rows_halo(grid_values, rim_depth)
    row_count = grid_values.shape[1]
    first_row = lax.axis_index("tile") * row_count - rim_depth
    domain_rows = row_count * lax.axis_size("tile")
    position = first_row + lax.iota(jnp.int32, row_count + 2 * rim_depth)
    inside = ((position >= 0) & (position < domain_rows)).astype(jnp.float32)[None, :, None]
    for pass_index in range(KSM):
        inside = inside[:, 1:-1]
        extended = (
            extended[:, 1:-1]
            + DIFFUSION * (extended[:, :-2] + extended[:, 2:] - 2.0 * extended[:, 1:-1])
        ) * inside
    return extended


def refine(extended):
    members_here, row_count, col_count = extended.shape
    lower_rows = extended[:, :-2]
    middle = extended[:, 1:-1]
    upper_rows = extended[:, 2:]
    pieces = []
    for offset in range(RATIO):
        shift_value = (offset + 0.5) / RATIO - 0.5
        if shift_value < 0:
            pieces.append((1.0 + shift_value) * middle - shift_value * lower_rows)
        else:
            pieces.append((1.0 - shift_value) * middle + shift_value * upper_rows)
    return jnp.stack(pieces, axis=2).reshape(members_here, (row_count - 2) * RATIO, col_count)


def refine_adjoint(fine_field):
    members_here, fine_count, col_count = fine_field.shape
    row_count = fine_count // RATIO
    blocks = fine_field.reshape(members_here, row_count, RATIO, col_count)
    middle = jnp.zeros_like(blocks[:, :, 0])
    lower_rows = jnp.zeros_like(middle)
    upper_rows = jnp.zeros_like(middle)
    for offset in range(RATIO):
        shift_value = (offset + 0.5) / RATIO - 0.5
        fine_layer = blocks[:, :, offset]
        if shift_value < 0:
            middle = middle + (1.0 + shift_value) * fine_layer
            lower_rows = lower_rows - shift_value * fine_layer
        else:
            middle = middle + (1.0 - shift_value) * fine_layer
            upper_rows = upper_rows + shift_value * fine_layer
    return (
        jnp.pad(middle, ((0, 0), (1, 1), (0, 0)))
        + jnp.pad(lower_rows, ((0, 0), (0, 2), (0, 0)))
        + jnp.pad(upper_rows, ((0, 0), (2, 0), (0, 0)))
    )


def forward(coarse, perturb, column_map):
    extended = smoothed(coarse, 1)
    members_here, row_count, coarse_cols = extended.shape
    mapped = jnp.dot(
        extended.astype(jnp.bfloat16).reshape(-1, coarse_cols),
        column_map,
        preferred_element_type=jnp.float32,
    )
    fine_field = refine(mapped.reshape(members_here, row_count, -1))
    member_term = jnp.sum(fine_field * perturb, axis=0)
    return lax.psum_scatter(member_term, "member", scatter_dimension=1, tiled=True)


def adjoint_map(spread_field, perturb, column_map):
    edge_terms = refine_adjoint(perturb * spread_field)
    rim_rows = jnp.stack([edge_terms[:, 0], edge_terms[:, -1]], axis=1)
    beside_all = rows_halo(rim_rows, 1)
    inner_rows = edge_terms[:, 1:-1]
    inner_rows = inner_rows.at[:, 0].add(beside_all[:, 0]).at[:, -1].add(beside_all[:, 3])
    members_here, row_count, fine_cols = inner_rows.shape
    pulled = lax.dot_general(
        inner_rows.astype(jnp.bfloat16).reshape(-1, fine_cols),
        column_map,
        (((1,), (1,)), ((), ())),
        preferred_element_type=jnp.float32,
    )
    return smoothed(pulled.reshape(members_here, row_count, -1), 0)


def bilinear_factors(index, row_frac, column_frac, region_width, row_count):
    row_pos = (index // region_width)[..., None]
    column_pos = (index % region_width)[..., None]
    row_ids = lax.broadcasted_iota(jnp.int32, index.shape + (row_count,), index.ndim)
    column_ids = lax.broadcasted_iota(jnp.int32, index.shape + (region_width,), index.ndim)
    row_factor = jnp.where(row_ids == row_pos, 1.0 - row_frac[..., None], 0.0) + jnp.where(
        row_ids == row_pos + 1, row_frac[..., None], 0.0
    )
    column_factor = jnp.where(
        column_ids == column_pos, 1.0 - column_frac[..., None], 0.0
    ) + jnp.where(column_ids == column_pos + 1, column_frac[..., None], 0.0)
    return (row_factor, column_factor)


def interpolate_region(field_region, index, row_frac, column_frac):
    row_count, region_width = field_region.shape
    row_factor, column_factor = bilinear_factors(
        index, row_frac, column_frac, region_width, row_count
    )
    along = jnp.einsum("bsr,rc->bsc", row_factor, field_region, precision=lax.Precision.HIGHEST)
    return jnp.sum(along * column_factor, axis=-1)


def spread_tile(residual, index, row_frac, column_frac, region_width, row_count):
    row_factor, column_factor = bilinear_factors(
        index, row_frac, column_frac, region_width, row_count
    )
    weighted = row_factor * residual[..., None]
    regions = jnp.einsum("bmsr,bmsc->rmc", weighted, column_factor, precision=lax.Precision.HIGHEST)
    return regions.reshape(row_count, -1)


def innovation(obs_state, obs_value, obs_error, instrument):
    bounded = jnp.tanh(obs_state)
    derivative = 1.0 + instrument * (1.0 - bounded * bounded)
    misfit = obs_state + instrument * bounded - obs_value
    precision_obs = 1.0 / (obs_error * obs_error)
    return (derivative * misfit * precision_obs, derivative * derivative * precision_obs)


def global_sum(values):
    return lax.psum(values, ("member", "tile"))


def shards(
    perturb,
    weights,
    column_map,
    background,
    stencil_index,
    row_fraction,
    column_fraction,
    block_lengths,
    obs_value,
    obs_error,
    instrument_gain,
):
    member_pos = lax.axis_index("member")
    member_count = lax.axis_size("member")
    tile_count = lax.axis_size("tile")
    fine_rows, region_width = background.shape
    local_index = stencil_index[0]
    local_row = row_fraction[0]
    local_col = column_fraction[0]
    slot_ids = lax.broadcasted_iota(jnp.int32, local_index.shape, 2)
    valid_slots = (slot_ids < block_lengths[0][:, :, None]).astype(jnp.float32)
    own_index = lax.dynamic_index_in_dim(local_index, member_pos, 1, False)
    own_row = lax.dynamic_index_in_dim(local_row, member_pos, 1, False)
    own_col = lax.dynamic_index_in_dim(local_col, member_pos, 1, False)
    own_valid = lax.dynamic_index_in_dim(valid_slots, member_pos, 1, False)

    def fan_out(values):
        arranged = jnp.transpose(values.reshape(member_count, tile_count, -1), (1, 0, 2))
        widened = jnp.broadcast_to(arranged[None], (member_count,) + arranged.shape)
        return widened.reshape(member_count * tile_count, member_count, -1)

    coarse = weights
    increment = forward(coarse, perturb, column_map)
    obs_state = interpolate_region(background + increment, own_index, own_row, own_col)
    received = lax.all_to_all(
        obs_state, ("member", "tile"), split_axis=0, concat_axis=0, tiled=True
    )
    residual, obs_weight = innovation(received, obs_value[0], obs_error[0], instrument_gain[0])
    residual, obs_weight = (
        lax.all_to_all(
            fan_out(residual), ("member", "tile"), split_axis=0, concat_axis=0, tiled=True
        ),
        lax.all_to_all(
            fan_out(obs_weight), ("member", "tile"), split_axis=0, concat_axis=0, tiled=True
        ),
    )
    spread_field = spread_tile(
        residual * valid_slots, local_index, local_row, local_col, region_width, fine_rows
    )
    gradient = coarse + adjoint_map(spread_field, perturb, column_map)
    grad_square = jnp.sum(gradient * gradient)
    grad_total = global_sum(grad_square)
    grad_image = forward(gradient, perturb, column_map)
    grad_obs = interpolate_region(grad_image, own_index, own_row, own_col)
    own_weight = lax.dynamic_index_in_dim(obs_weight, member_pos, 1, False)
    curvature = jnp.sum(own_valid * own_weight * grad_obs * grad_obs)
    curve_total = global_sum(curvature)
    step_size = grad_total / (grad_total + curve_total)
    coarse = coarse - step_size * gradient
    increment = increment - step_size * grad_image
    return (coarse, increment)


def solution(mesh):
    placed = (
        P("member", "tile", None),
        P("member", "tile", None),
        P(),
        P("tile", "member"),
        P("tile", None, None, None),
        P("tile", None, None, None),
        P("tile", None, None, None),
        P("tile", None, None),
        P(("member", "tile"), None, None),
        P(("member", "tile"), None, None),
        P(("member", "tile")),
    )
    return jax.shard_map(
        shards,
        mesh=mesh,
        in_specs=placed,
        out_specs=(P("member", "tile", None), P("tile", "member")),
        check_vma=False,
    )
```

profile of v0, /device:TPU:0, one launch (start us, length us, event | category | flops | bytes accessed | tf_op | source)
XLA Modules:
  0.0 213.4 jit_solution(5404511777827200009)
XLA Ops:
  8.3 4.9 %collective-permute-start = (f32[16,4,1280]{2,0,1:T(8,128)S(1)}, f32[16,4,1280]{2,0,1:T(8,128)S(1)}, u32[]{:S(2)}, u32[]{:S(2)}) collective-permute-start(f32[16,4,1280]{2,0,1:T(8,128)S(1)} %copy.82), channel_id=1, source_target_pairs={{0,1},{1,2},{2,3},{3,4},{4,5},{5,6},{6,7},{8,9},{9,10},{10,11},{11... | collective-permute-start | bytes 983048 | tf_op jit(solution)/shard_map/ppermute | solution.py:18
  13.1 1.3 collective-permute-start.1
  16.9 10.2 %collective-permute-done = f32[16,4,1280]{2,0,1:T(8,128)S(1)} collective-permute-done((f32[16,4,1280]{2,0,1:T(8,128)S(1)}, f32[16,4,1280]{2,0,1:T(8,128)S(1)}, u32[]{:S(2)}, u32[]{:S(2)}) %collective-permute-start) | collective-permute-done | bytes 327712 | tf_op jit(solution)/shard_map/ppermute | solution.py:18
  28.5 2.5 %copy-done = bf16[1280,2560]{1,0:T(8,128)(2,1)S(1)} copy-done((bf16[1280,2560]{1,0:T(8,128)(2,1)S(1)}, bf16[1280,2560]{1,0:T(8,128)(2,1)}, u32[]{:S(2)}) %copy-start) | copy-done | bytes 6553624
  31.0 1.2 fusion.4
  34.0 2.0 fusion.6
  36.6 20.5 %reduce-scatter.3.cloned.1.call-done = f32[16,640]{1,0:T(8,128)} async-done(((f32[16,2560]{1,0:T(8,128)}), f32[16,640]{1,0:T(8,128)}) %reduce-scatter.3.cloned.1.call-update) | async-done | bytes 40976 | tf_op jit(solution)/shard_map/reduce_scatter | solution.py:95
  57.1 2.3 %fusion.17 = f32[32,8]{1,0:T(8,128)} fusion(f32[32,8]{1,0:T(8,128)S(1)} %copy.65, s32[32,8]{1,0:T(8,128)S(1)} %copy.64, f32[32,8]{1,0:T(8,128)S(1)} %copy.63, s32[32,8]{1,0:T(8,128)S(1)} %copy.62, f32[32,8]{1,0:T(8,128)S(1)} %copy.57, s32[32,8]{1,0:T(8,128)S(1)} %copy.56, f32[32,8]{1,0:T(8,128)S(1)} %copy.55, s32[32,8]{1,0:T(8,128)S(1)} %copy.54, ...), kind=kOutput, calls=%fused_computation.26 | convolution fusion | flops 32634624 | bytes 91136 | tf_op jit(solution)/shard_map/bsr,rc->bsc/dot_general | solution.py:133
  59.3 4.6 %all-to-all-start = ((f32[32,1,8]{2,1,0:T(1,128)}), f32[32,1,8]{2,1,0:T(1,128)S(1)}, u32[]{:S(2)}, u32[]{:S(2)}) async-start(f32[32,1,8]{2,1,0:T(1,128)} %bitcast.23), calls=%async_computation.1 | async-start | bytes 32768 | tf_op jit(solution)/shard_map/all_to_all | solution.py:193
  64.8 6.2 %all-to-all-done = f32[32,1,8]{2,1,0:T(1,128)S(1)} async-done(((f32[32,1,8]{2,1,0:T(1,128)}), f32[32,1,8]{2,1,0:T(1,128)S(1)}, u32[]{:S(2)}, u32[]{:S(2)}) %all-to-all-start) | async-done | bytes 1056 | tf_op jit(solution)/shard_map/all_to_all | solution.py:193
  71.6 2.6 %all-to-all-start.1 = ((f32[32,4,8]{2,1,0:T(4,128)}), f32[32,4,8]{2,1,0:T(4,128)S(1)}, u32[]{:S(2)}, u32[]{:S(2)}) async-start(f32[32,4,8]{2,1,0:T(4,128)} %bitcast.27), calls=%async_computation.2 | async-start | bytes 131072 | tf_op jit(solution)/shard_map/all_to_all | solution.py:198
  74.3 7.2 %all-to-all-done.1 = f32[32,4,8]{2,1,0:T(4,128)S(1)} async-done(((f32[32,4,8]{2,1,0:T(4,128)}), f32[32,4,8]{2,1,0:T(4,128)S(1)}, u32[]{:S(2)}, u32[]{:S(2)}) %all-to-all-start.1) | async-done | bytes 4128 | tf_op jit(solution)/shard_map/all_to_all | solution.py:198
  81.7 2.8 %fusion.19 = f32[4,2,8,640]{3,2,1,0:T(8,128)S(1)} fusion(f32[32,4,8]{0,2,1:T(8,128)S(1)} %bitcast.189, s32[32,4,8]{0,2,1:T(8,128)S(1)} %get-tuple-element.63, f32[32,4,8]{0,2,1:T(8,128)S(1)} %get-tuple-element.70, s32[32,4,8]{0,2,1:T(8,128)S(1)} %get-tuple-element.64, f32[32,4,8]{0,2,1:T(8,128)S(1)} %copy.71, f32[32,4,8]{0,2,1:T(8,128)S(1)} %bitcast.190, ...), kind=kOutput, calls=%fused_computation.28 | convolution fusion | flops 129204224 | bytes 200704 | tf_op jit(solution)/shard_map/bmsr,bmsc->rmc/dot_general | solution.py:142
  85.7 2.8 %collective-permute-start.2 = (f32[16,1,2560]{2,0,1:T(8,128)S(1)}, f32[16,1,2560]{2,0,1:T(8,128)S(1)}, u32[]{:S(2)}, u32[]{:S(2)}) collective-permute-start(f32[16,1,2560]{2,0,1:T(8,128)S(1)} %get-tuple-element.48), channel_id=1, source_target_pairs={{0,1},{1,2},{2,3},{3,4},{4,5},{5,6},{6,7},{8,9},{9,10},{10,11},{11... | collective-permute-start | bytes 491528 | tf_op jit(solution)/shard_map/ppermute | solution.py:18
  88.7 1.3 collective-permute-start.3
  90.0 2.2 %collective-permute-done.2 = f32[16,1,2560]{2,0,1:T(8,128)S(1)} collective-permute-done((f32[16,1,2560]{2,0,1:T(8,128)S(1)}, f32[16,1,2560]{2,0,1:T(8,128)S(1)}, u32[]{:S(2)}, u32[]{:S(2)}) %collective-permute-start.2) | collective-permute-done | bytes 163872 | tf_op jit(solution)/shard_map/ppermute | solution.py:18
  92.3 4.3 %collective-permute-done.3 = f32[16,1,2560]{2,0,1:T(8,128)S(1)} collective-permute-done((f32[16,1,2560]{2,0,1:T(8,128)S(1)}, f32[16,1,2560]{2,0,1:T(8,128)S(1)}, u32[]{:S(2)}, u32[]{:S(2)}) %collective-permute-start.3) | collective-permute-done | bytes 163872 | tf_op jit(solution)/shard_map/ppermute | solution.py:21
  96.6 2.1 fusion.2
  98.7 1.3 collective-permute-start.5
  100.0 4.6 %collective-permute-start.4 = (f32[16,3,1280]{2,0,1:T(8,128)S(1)}, f32[16,3,1280]{2,0,1:T(8,128)S(1)}, u32[]{:S(2)}, u32[]{:S(2)}) collective-permute-start(f32[16,3,1280]{2,0,1:T(8,128)S(1)} %get-tuple-element.57), channel_id=1, source_target_pairs={{0,1},{1,2},{2,3},{3,4},{4,5},{5,6},{6,7},{8,9},{9,10},{10,11},{11... | collective-permute-start | bytes 737288 | tf_op jit(solution)/shard_map/ppermute | solution.py:18
  104.7 3.0 %collective-permute-done.5 = f32[16,3,1280]{2,0,1:T(8,128)S(1)} collective-permute-done((f32[16,3,1280]{2,0,1:T(8,128)S(1)}, f32[16,3,1280]{2,0,1:T(8,128)S(1)}, u32[]{:S(2)}, u32[]{:S(2)}) %collective-permute-start.5) | collective-permute-done | bytes 245792 | tf_op jit(solution)/shard_map/ppermute | solution.py:21
  107.7 5.5 %collective-permute-done.4 = f32[16,3,1280]{2,0,1:T(8,128)S(1)} collective-permute-done((f32[16,3,1280]{2,0,1:T(8,128)S(1)}, f32[16,3,1280]{2,0,1:T(8,128)S(1)}, u32[]{:S(2)}, u32[]{:S(2)}) %collective-permute-start.4) | collective-permute-done | bytes 245792 | tf_op jit(solution)/shard_map/ppermute | solution.py:18
  115.1 1.3 collective-permute-start.7
  116.4 5.0 %collective-permute-start.6 = (f32[16,4,1280]{2,0,1:T(8,128)S(1)}, f32[16,4,1280]{2,0,1:T(8,128)S(1)}, u32[]{:S(2)}, u32[]{:S(2)}) collective-permute-start(f32[16,4,1280]{2,0,1:T(8,128)S(1)} %get-tuple-element.35), channel_id=1, source_target_pairs={{0,1},{1,2},{2,3},{3,4},{4,5},{5,6},{6,7},{8,9},{9,10},{10,11},{11... | collective-permute-start | bytes 983048 | tf_op jit(solution)/shard_map/ppermute | solution.py:18
  122.0 3.8 %all-to-all-start.2 = ((f32[32,4,8]{2,1,0:T(4,128)}), f32[32,4,8]{2,1,0:T(4,128)S(1)}, u32[]{:S(2)}, u32[]{:S(2)}) async-start(f32[32,4,8]{2,1,0:T(4,128)} %bitcast.39), calls=%async_computation.3 | async-start | bytes 131072 | tf_op jit(solution)/shard_map/all_to_all | solution.py:201
  126.1 1.2 collective-permute-done.7
  127.3 7.8 %collective-permute-done.6 = f32[16,4,1280]{2,0,1:T(8,128)S(1)} collective-permute-done((f32[16,4,1280]{2,0,1:T(8,128)S(1)}, f32[16,4,1280]{2,0,1:T(8,128)S(1)}, u32[]{:S(2)}, u32[]{:S(2)}) %collective-permute-start.6) | collective-permute-done | bytes 327712 | tf_op jit(solution)/shard_map/ppermute | solution.py:18
  135.5 4.1 %fusion = f32[16,6,2560]{2,0,1:T(8,128)S(1)} fusion(bf16[1280,2560]{1,0:T(8,128)(2,1)} %param.17, f32[16,8,1280]{2,0,1:T(8,128)S(1)} %fusion.33, f32[6]{0:T(128)S(1)} %slice_bitcast_fusion.7), kind=kOutput, calls=%fused_computation | convolution fusion | flops 630005760 | bytes 9011712 | tf_op jit(solution)/shard_map/dot_general | solution.py:88
  140.4 2.0 fusion.7
  142.6 18.5 %reduce-scatter.5.cloned.1.call-done = f32[16,640]{1,0:T(8,128)} async-done(((f32[16,2560]{1,0:T(8,128)}), f32[16,640]{1,0:T(8,128)}) %reduce-scatter.5.cloned.1.call-update) | async-done | bytes 40976 | tf_op jit(solution)/shard_map/reduce_scatter | solution.py:95
  161.1 1.7 fusion.18
  163.4 39.6 %all-reduce.3 = (f32[]{:T(128)}, f32[]{:T(128)}) all-reduce(f32[]{:T(128)} %get-tuple-element.34, f32[]{:T(128)} %fusion.95), channel_id=1, replica_groups=mesh['member'=4,'tile'=8] {'member','tile'}, use_global_device_ids=true, to_apply=%region_4.5 | all-reduce | flops 2 | bytes 16 | tf_op jit(solution)/shard_map/psum | solution.py:155
  (96 shorter events, 16.1 us)
Async XLA Ops:
  7.2 49.9 %reduce-scatter.3.cloned.1.call-start = ((), (), s32[]{:S(2)}) async-start(), calls=%async_computation.5 | async-start | bytes 204800 | tf_op jit(solution)/shard_map/reduce_scatter | solution.py:95
  8.3 18.8 %collective-permute-start = (f32[16,4,1280]{2,0,1:T(8,128)S(1)}, f32[16,4,1280]{2,0,1:T(8,128)S(1)}, u32[]{:S(2)}, u32[]{:S(2)}) collective-permute-start(f32[16,4,1280]{2,0,1:T(8,128)S(1)} %copy.82), channel_id=1, source_target_pairs={{0,1},{1,2},{2,3},{3,4},{4,5},{5,6},{6,7},{8,9},{9,10},{10,11},{11... | collective-permute-start | bytes 983048 | tf_op jit(solution)/shard_map/ppermute | solution.py:18
  13.1 15.0 %collective-permute-start.1 = (f32[16,4,1280]{2,0,1:T(8,128)S(1)}, f32[16,4,1280]{2,0,1:T(8,128)S(1)}, u32[]{:S(2)}, u32[]{:S(2)}) collective-permute-start(f32[16,4,1280]{2,0,1:T(8,128)S(1)} %copy.82), channel_id=1, source_target_pairs={{1,0},{2,1},{3,2},{4,3},{5,4},{6,5},{7,6},{9,8},{10,9},{11,10},{12... | collective-permute-start | bytes 983048 | tf_op jit(solution)/shard_map/ppermute | solution.py:21
  28.1 2.9 %copy-start = (bf16[1280,2560]{1,0:T(8,128)(2,1)S(1)}, bf16[1280,2560]{1,0:T(8,128)(2,1)}, u32[]{:S(2)}) copy-start(bf16[1280,2560]{1,0:T(8,128)(2,1)} %param.17) | copy-start | bytes 19660804
  32.7 1.3 copy-start.1
  34.0 2.0 copy-start.5
  34.0 23.1 %copy-start.10 = (f32[16,640]{1,0:T(8,128)S(1)}, f32[16,640]{1,0:T(8,128)}, u32[]{:S(2)}) copy-start(f32[16,640]{1,0:T(8,128)} %param.18) | copy-start | bytes 122884
  34.0 30.7 %copy-start.9 = (f32[1,32,8]{1,2,0:T(8,128)S(1)}, f32[1,32,8]{1,2,0:T(8,128)}, u32[]{:S(2)}) copy-start(f32[1,32,8]{1,2,0:T(8,128)} %param.23) | copy-start | bytes 3076
  34.0 47.5 %copy-start.8 = (s32[1,32,4]{1,2,0:T(4,128)S(1)}, s32[1,32,4]{1,2,0:T(4,128)}, u32[]{:S(2)}) copy-start(s32[1,32,4]{1,2,0:T(4,128)} %param.22) | copy-start | bytes 1540
  35.9 45.7 %copy-start.6 = (f32[1,32,4,8]{1,3,2,0:T(8,128)S(1)}, f32[1,32,4,8]{1,3,2,0:T(8,128)}, u32[]{:S(2)}) copy-start(f32[1,32,4,8]{1,3,2,0:T(8,128)} %param.21) | copy-start | bytes 12292
  35.9 45.7 %copy-start.7 = (f32[1,32,4,8]{1,3,2,0:T(8,128)S(1)}, f32[1,32,4,8]{1,3,2,0:T(8,128)}, u32[]{:S(2)}) copy-start(f32[1,32,4,8]{1,3,2,0:T(8,128)} %param.20) | copy-start | bytes 12292
  59.3 11.6 %all-to-all-start = ((f32[32,1,8]{2,1,0:T(1,128)}), f32[32,1,8]{2,1,0:T(1,128)S(1)}, u32[]{:S(2)}, u32[]{:S(2)}) async-start(f32[32,1,8]{2,1,0:T(1,128)} %bitcast.23), calls=%async_computation.1 | async-start | bytes 32768 | tf_op jit(solution)/shard_map/all_to_all | solution.py:193
  71.6 9.9 %all-to-all-start.1 = ((f32[32,4,8]{2,1,0:T(4,128)}), f32[32,4,8]{2,1,0:T(4,128)S(1)}, u32[]{:S(2)}, u32[]{:S(2)}) async-start(f32[32,4,8]{2,1,0:T(4,128)} %bitcast.27), calls=%async_computation.2 | async-start | bytes 131072 | tf_op jit(solution)/shard_map/all_to_all | solution.py:198
  84.5 12.1 %slice-start = ((s8[6553600]{0:T(1024)(128)(4,1)}), s8[4194304]{0:T(1024)(128)(4,1)S(1)}, s32[]{:S(2)}) async-start(s8[6553600]{0:T(1024)(128)(4,1)} %bitcast.183), calls=%async_computation.7 | async-start | bytes 8388608
  85.6 10.9 %slice-start.1 = ((s8[6553600]{0:T(1024)(128)(4,1)}), s8[2359296]{0:T(1024)(128)(4,1)S(1)}, s32[]{:S(2)}) async-start(s8[6553600]{0:T(1024)(128)(4,1)} %bitcast.183), calls=%async_computation.8 | async-start | bytes 4718592
  85.7 6.5 %collective-permute-start.2 = (f32[16,1,2560]{2,0,1:T(8,128)S(1)}, f32[16,1,2560]{2,0,1:T(8,128)S(1)}, u32[]{:S(2)}, u32[]{:S(2)}) collective-permute-start(f32[16,1,2560]{2,0,1:T(8,128)S(1)} %get-tuple-element.48), channel_id=1, source_target_pairs={{0,1},{1,2},{2,3},{3,4},{4,5},{5,6},{6,7},{8,9},{9,10},{10,11},{11... | collective-permute-start | bytes 491528 | tf_op jit(solution)/shard_map/ppermute | solution.py:18
  88.7 7.8 %collective-permute-start.3 = (f32[16,1,2560]{2,0,1:T(8,128)S(1)}, f32[16,1,2560]{2,0,1:T(8,128)S(1)}, u32[]{:S(2)}, u32[]{:S(2)}) collective-permute-start(f32[16,1,2560]{2,0,1:T(8,128)S(1)} %get-tuple-element.47), channel_id=1, source_target_pairs={{1,0},{2,1},{3,2},{4,3},{5,4},{6,5},{7,6},{9,8},{10,9},{11,10},{12... | collective-permute-start | bytes 491528 | tf_op jit(solution)/shard_map/ppermute | solution.py:21
  98.7 9.0 %collective-permute-start.5 = (f32[16,3,1280]{2,0,1:T(8,128)S(1)}, f32[16,3,1280]{2,0,1:T(8,128)S(1)}, u32[]{:S(2)}, u32[]{:S(2)}) collective-permute-start(f32[16,3,1280]{2,0,1:T(8,128)S(1)} %get-tuple-element.58), channel_id=1, source_target_pairs={{1,0},{2,1},{3,2},{4,3},{5,4},{6,5},{7,6},{9,8},{10,9},{11,10},{12... | collective-permute-start | bytes 737288 | tf_op jit(solution)/shard_map/ppermute | solution.py:21
  100.0 13.2 %collective-permute-start.4 = (f32[16,3,1280]{2,0,1:T(8,128)S(1)}, f32[16,3,1280]{2,0,1:T(8,128)S(1)}, u32[]{:S(2)}, u32[]{:S(2)}) collective-permute-start(f32[16,3,1280]{2,0,1:T(8,128)S(1)} %get-tuple-element.57), channel_id=1, source_target_pairs={{0,1},{1,2},{2,3},{3,4},{4,5},{5,6},{6,7},{8,9},{9,10},{10,11},{11... | collective-permute-start | bytes 737288 | tf_op jit(solution)/shard_map/ppermute | solution.py:18
  113.3 1.0 copy-start.2
  115.1 12.3 %collective-permute-start.7 = (f32[16,4,1280]{2,0,1:T(8,128)S(1)}, f32[16,4,1280]{2,0,1:T(8,128)S(1)}, u32[]{:S(2)}, u32[]{:S(2)}) collective-permute-start(f32[16,4,1280]{2,0,1:T(8,128)S(1)} %get-tuple-element.35), channel_id=1, source_target_pairs={{1,0},{2,1},{3,2},{4,3},{5,4},{6,5},{7,6},{9,8},{10,9},{11,10},{12... | collective-permute-start | bytes 983048 | tf_op jit(solution)/shard_map/ppermute | solution.py:21
  116.4 18.8 %collective-permute-start.6 = (f32[16,4,1280]{2,0,1:T(8,128)S(1)}, f32[16,4,1280]{2,0,1:T(8,128)S(1)}, u32[]{:S(2)}, u32[]{:S(2)}) collective-permute-start(f32[16,4,1280]{2,0,1:T(8,128)S(1)} %get-tuple-element.35), channel_id=1, source_target_pairs={{0,1},{1,2},{2,3},{3,4},{4,5},{5,6},{6,7},{8,9},{9,10},{10,11},{11... | collective-permute-start | bytes 983048 | tf_op jit(solution)/shard_map/ppermute | solution.py:18
  122.0 20.5 %all-to-all-start.2 = ((f32[32,4,8]{2,1,0:T(4,128)}), f32[32,4,8]{2,1,0:T(4,128)S(1)}, u32[]{:S(2)}, u32[]{:S(2)}) async-start(f32[32,4,8]{2,1,0:T(4,128)} %bitcast.39), calls=%async_computation.3 | async-start | bytes 131072 | tf_op jit(solution)/shard_map/all_to_all | solution.py:201
  125.9 35.2 %reduce-scatter.5.cloned.1.call-start = ((), (), s32[]{:S(2)}) async-start(), calls=%async_computation.6 | async-start | bytes 204800 | tf_op jit(solution)/shard_map/reduce_scatter | solution.py:95
  142.4 63.6 %copy-start.3 = (f32[16,640]{1,0:T(8,128)S(1)}, f32[16,640]{1,0:T(8,128)}, u32[]{:S(2)}) copy-start(f32[16,640]{1,0:T(8,128)} %reduce-scatter.3.cloned.1.call-done) | copy-start | bytes 122884
  161.1 44.9 %copy-start.4 = (f32[16,640]{1,0:T(8,128)S(1)}, f32[16,640]{1,0:T(8,128)}, u32[]{:S(2)}) copy-start(f32[16,640]{1,0:T(8,128)} %reduce-scatter.5.cloned.1.call-done) | copy-start | bytes 122884
Sparse Core Ops, SparseCore 0:
  36.1 20.9 reduce-scatter.2
  142.6 18.4 reduce-scatter.4
where the time goes:
time: 214 us; the launch traced here: 213 us
  waiting for transfers between devices  86.7 us (41%)
  blocking collectives  39.6 us (19%)
  starting transfers between devices  33.7 us (16%)
  between operations  17.1 us (8%)
  matrix products  14.1 us (7%)
  other arithmetic  11.8 us (6%)
  local copies, waits for them, and re-layouts  10.5 us (5%)
    psum x1, blocking collectives, global_sum(): return lax.psum(values, ('member', 'tile'))  39.6 us
    reduce_scatter x2, waiting for transfers between devices, forward(): lax.psum_scatter(member_term, 'member', scatter_dimension=1, tiled=True)  39 us
    ppermute x4, waiting for transfers between devices, padded(): lax.ppermute(lax.slice_in_dim(block, block.shape[dim] - width, None, axis...  25.8 us
    ppermute x4, starting transfers between devices, padded(): lax.ppermute(lax.slice_in_dim(block, block.shape[dim] - width, None, axis...  17.3 us
    ppermute x4, waiting for transfers between devices, padded(): lax.ppermute(lax.slice_in_dim(block, 0, width, axis=dim), axis, backward)  8.47 us
    unnamed x30, local copies, waits for them, and re-layouts  7.32 us
    all_to_all x1, waiting for transfers between devices, shards(): lax.all_to_all(fan_out(residual), ('member', 'tile'), split_axis=0, conca...  7.2 us
    all_to_all x1, waiting for transfers between devices, shards(): lax.all_to_all(obs_state, ('member', 'tile'), split_axis=0, concat_axis=0...  6.21 us
  transfers between devices with their start and end apart: 13, of which 11 were waited for; matrix products, arithmetic and copies ran while one was open for 6% of the time, Pallas kernels for 0%

commit v1 on v0

v1 whole, which is shorter than its diff:
```python
import functools

import jax
import jax.numpy as jnp
from jax import lax
from jax.experimental import pallas as pl
from jax.experimental.pallas import tpu as pltpu
from jax.sharding import PartitionSpec as P

RATIO = 4
KSM = 3
DIFFUSION = 0.45
BLOCK = 256
LANES = 128
MESH = pl.DeviceIdType.MESH
F32 = jnp.float32
BF16 = jnp.bfloat16


def sweep(rows, first, mask_of):
    for _ in range(KSM):
        first += 1
        inner = []
        for at in range(1, len(rows) - 1):
            mid = rows[at]
            new = mid + DIFFUSION * (rows[at - 1] + rows[at + 1] - 2.0 * mid)
            mask = mask_of(first + at - 1)
            inner.append(new if mask is None else new * mask)
        rows = inner
    return rows


def split_rows(values):
    high = values.astype(BF16)
    low = (values - high.astype(F32)).astype(BF16)
    return jnp.concatenate([high, low], axis=0)


def kernel(
    members,
    tiles,
    pay_ref,
    w_ref,
    obs_ref,
    bg_ref,
    map_hbm,
    per_hbm,
    outw_ref,
    outi_ref,
    cmap,
    per,
    hot,
    rowf,
    fields,
    obsin,
    wsend,
    halo,
    acc,
    flat,
    part,
    frecv,
    hsend,
    hrecv,
    ssend,
    srecv,
    spread,
    edges,
    pown,
    psend,
    precv,
    grad,
    load_sem,
    o1_send,
    o1_recv,
    o2_send,
    o2_recv,
    w_send,
    w_recv,
    h_send,
    h_recv,
    f_send,
    f_recv,
    p_send,
    p_recv,
    s_send,
    s_recv,
):
    m = lax.axis_index("member")
    t = lax.axis_index("tile")
    chunks, rows, mem, width = w_ref.shape
    region = bg_ref.shape[1]
    fine_rows = bg_ref.shape[0]
    slots = obs_ref.shape[2]
    fine_cols = cmap.shape[1]
    ext = rows + 2
    cap = slots // (members * tiles)
    scalar_row = hsend.shape[1] - 8

    load_map = pltpu.make_async_copy(map_hbm, cmap, load_sem.at[0])
    load_per = pltpu.make_async_copy(per_hbm, per, load_sem.at[1])
    load_map.start()
    load_per.start()

    barrier = pltpu.get_barrier_semaphore()
    for d in range(1, members):
        pl.semaphore_signal(
            barrier, inc=1, device_id=(lax.rem(m + d, members), t), device_id_type=MESH
        )
    for d in range(1, tiles):
        pl.semaphore_signal(
            barrier, inc=1, device_id=(m, lax.rem(t + d, tiles)), device_id_type=MESH
        )

    wsend[...] = w_ref[...].astype(BF16)
    obsin[m, t] = pay_ref[t]
    pl.semaphore_wait(barrier, members + tiles - 2)

    def remote(src, dst, ssem, rsem, where):
        return pltpu.make_async_remote_copy(
            src_ref=src, dst_ref=dst, send_sem=ssem, recv_sem=rsem, device_id=where, device_id_type=MESH
        )

    def halo_copy(side, j):
        target = jnp.clip(t + 1 - 2 * side, 0, tiles - 1)
        return remote(
            wsend.at[j], halo.at[side, j], w_send.at[side, j], w_recv.at[side, j], (m, target)
        )

    def has_target(step):
        return (t + step >= 0) & (t + step < tiles)

    def first_obs(d):
        to = lax.rem(t + d, tiles)
        return remote(pay_ref.at[to], obsin.at[m, t], o1_send.at[d], o1_recv.at[d], (m, to))

    def second_obs(d):
        to = lax.rem(m + d, members)
        return remote(obsin.at[m], obsin.at[m], o2_send.at[d], o2_recv.at[d], (to, t))

    for d in range(1, tiles):
        first_obs(d).start()

    def send_halo(j, carry):
        for side in range(2):

            @pl.when(has_target(1 - 2 * side))
            def _():
                halo_copy(side, j).start()

        return carry

    lax.fori_loop(0, chunks, send_halo, 0)

    for side in range(2):

        @pl.when(jnp.logical_not(has_target(2 * side - 1)))
        def _():
            halo[side] = jnp.zeros(halo.shape[1:], halo.dtype)

    shifts = (-1, 1, -2, 2)
    for at, shift in enumerate(shifts):

        @pl.when(jnp.logical_not(has_target(shift)))
        def _():
            precv[at] = jnp.zeros(precv.shape[1:], precv.dtype)

    hsend[...] = jnp.zeros(hsend.shape, hsend.dtype)

    def prepare(k, carry):
        info = obs_ref[k]
        row_pos, col_pos, row_frac = info[0:1], info[1:2], info[2:3]
        col_ids = lax.broadcasted_iota(jnp.int32, (region, slots), 0).astype(F32)
        hot[k, :, 0:slots] = jnp.where(col_ids == col_pos, 1.0, 0.0).astype(BF16)
        hot[k, :, slots : 2 * slots] = jnp.where(col_ids == col_pos + 1.0, 1.0, 0.0).astype(BF16)
        row_ids = lax.broadcasted_iota(jnp.int32, (fine_rows, slots), 0).astype(F32)
        rowf[k] = jnp.where(row_ids == row_pos, 1.0 - row_frac, 0.0) + jnp.where(
            row_ids == row_pos + 1.0, row_frac, 0.0
        )
        return carry

    lax.fori_loop(0, members, prepare, 0)

    for d in range(1, tiles):
        first_obs(d).wait_recv()
    for d in range(1, members):
        second_obs(d).start()

    low1 = jnp.where(t > 0, 1.0, 0.0).astype(F32)
    high1 = jnp.where(t < tiles - 1, 1.0, 0.0).astype(F32)
    low2 = jnp.where(t > 1, 1.0, 0.0).astype(F32)
    high2 = jnp.where(t < tiles - 2, 1.0, 0.0).astype(F32)

    def mask_of(row):
        if row < -rows:
            return low2
        if row < 0:
            return low1
        if row < rows:
            return None
        if row < 2 * rows:
            return high1
        return high2

    def extended_weights(j, at):
        cols = pl.ds(at * LANES, LANES)
        return (
            [halo[0, j, r, :, cols].astype(F32) for r in range(rows)]
            + [w_ref[j, r, :, cols] for r in range(rows)]
            + [halo[1, j, r, :, cols].astype(F32) for r in range(rows)]
        )

    def map_chunk(j, lhs):
        depth = pl.ds(pl.multiple_of(j * width, width), width)
        product = jnp.dot(lhs, cmap[depth, :], preferred_element_type=F32)

        @pl.when(j == 0)
        def _():
            acc[...] = product

        @pl.when(j > 0)
        def _():
            acc[...] += product

    def smooth_to_lhs(pieces):
        return jnp.concatenate(
            [
                jnp.concatenate([piece[r] for piece in pieces], axis=1).astype(BF16)
                for r in range(ext)
            ],
            axis=0,
        )

    def first_forward(j, carry):
        for side in range(2):

            @pl.when(has_target(2 * side - 1))
            def _():
                halo_copy(side, j).wait_recv()

        map_chunk(
            j,
            smooth_to_lhs(
                [sweep(extended_weights(j, at), -rows, mask_of) for at in range(width // LANES)]
            ),
        )
        return carry

    load_map.wait()
    load_per.wait()
    lax.fori_loop(0, chunks, first_forward, 0)

    weights_of = []
    for offset in range(RATIO):
        shift = (offset + 0.5) / RATIO - 0.5
        weights_of.append((1.0 - abs(shift), abs(shift), -1 if shift < 0 else 1))

    def member_sum(block, carry):
        cols = pl.ds(pl.multiple_of(block * LANES, LANES), LANES)
        mapped = [acc[pl.ds(i * mem, mem), cols] for i in range(ext)]
        lines = []
        for i in range(rows):
            for offset in range(RATIO):
                near, far, side = weights_of[offset]
                fine = near * mapped[i + 1] + far * mapped[i + 1 + side]
                term = fine * per[RATIO * i + offset, :, cols].astype(F32)
                lines.append(jnp.sum(term, axis=0, keepdims=True))
        flat[:, cols] = jnp.concatenate(lines, axis=0)
        return carry

    def part_copy(which, d):
        to = lax.rem(m + d, members)
        return remote(
            part.at[which, to], frecv.at[which, m], f_send.at[which, d], f_recv.at[which, d], (to, t)
        )

    def h_copy(which, d):
        to = lax.rem(m + d, members)
        return remote(
            hsend.at[which], hrecv.at[which, m], h_send.at[which, d], h_recv.at[which, d], (to, t)
        )

    def observe(which, scale):
        lax.fori_loop(0, fine_cols // LANES, member_sum, 0)
        for k in range(members):
            field = flat[:, k * region : (k + 1) * region]
            part[which, k] = field
            if which == 0:
                field = field + bg_ref[...] * jnp.where(m == k, 1.0, 0.0).astype(F32)
            found = jnp.dot(split_rows(field), hot[k], preferred_element_type=F32)
            found = found[:fine_rows] + found[fine_rows:]
            col_frac = obs_ref[k][3:4]
            along = (1.0 - col_frac) * found[:, :slots] + col_frac * found[:, slots:]
            hsend[which, k : k + 1, :] = jnp.sum(along * rowf[k], axis=0, keepdims=True)
        for d in range(1, members):
            h_copy(which, d).start()
        for d in range(1, members):
            part_copy(which, d).start()

    def gathered(which):
        hrecv[which, m] = hsend[which]
        for d in range(1, members):
            h_copy(which, d).wait_recv()
        total = hrecv[which, 0]
        for k in range(1, members):
            total = total + hrecv[which, k]
        return total

    observe(0, None)

    for d in range(1, members):
        second_obs(d).wait_recv()
    listed = obsin[...].reshape(members * tiles * 8, LANES)
    owner_ids = lax.broadcasted_iota(jnp.int32, (members * tiles, 8, slots), 0)
    lane_ids = lax.broadcasted_iota(jnp.int32, (members * tiles, 8, slots), 2)
    chosen = lane_ids // cap == owner_ids
    source = lax.broadcasted_iota(jnp.int32, (LANES, slots), 0)
    target = lax.broadcasted_iota(jnp.int32, (LANES, slots), 1)
    for k in range(members):
        pick = jnp.where(source == k * cap + target % cap, 1.0, 0.0).astype(F32)
        wide = jnp.dot(listed, pick, precision=lax.Precision.HIGHEST, preferred_element_type=F32)
        wide = wide.reshape(members * tiles, 8, slots)
        fields[k] = jnp.sum(jnp.where(chosen, wide, 0.0), axis=0)

    state = gathered(0)

    for k in range(members):
        value, error, gain = fields[k][0:1], fields[k][1:2], fields[k][2:3]
        here = state[k : k + 1]
        bounded = jnp.tanh(here)
        slope = 1.0 + gain * (1.0 - bounded * bounded)
        precision = 1.0 / (error * error)
        live = obs_ref[k][4:5]
        residual = slope * (here + gain * bounded - value) * precision * live
        fields[k, 3:4] = slope * slope * precision * live
        col_frac = obs_ref[k][3:4]
        weighted = rowf[k] * residual
        both = jnp.concatenate([weighted * (1.0 - col_frac), weighted * col_frac], axis=1)
        found = lax.dot_general(
            split_rows(both), hot[k], (((1,), (1,)), ((), ())), preferred_element_type=F32
        )
        spread[:, k * region : (k + 1) * region] = found[:fine_rows] + found[fine_rows:]

    def adjoint_terms(block, carry):
        cols = pl.ds(pl.multiple_of(block * LANES, LANES), LANES)
        here = spread[:, cols]
        terms = [None] * ext

        def add(at, value):
            terms[at] = value if terms[at] is None else terms[at] + value

        for i in range(rows):
            for offset in range(RATIO):
                near, far, side = weights_of[offset]
                r = RATIO * i + offset
                layer = per[r, :, cols].astype(F32) * here[r : r + 1]
                add(i + 1, near * layer)
                add(i + 1 + side, far * layer)
        for at in range(ext):
            edges[pl.ds(at * mem, mem), cols] = terms[at].astype(BF16)
        return carry

    lax.fori_loop(0, fine_cols // LANES, adjoint_terms, 0)

    spans = {-1: (0, ext), 1: (0, ext), -2: (ext - rows, ext), 2: (0, rows)}

    def pulled_copy(at, j):
        shift = shifts[at]
        begin, end = spans[shift]
        to = jnp.clip(t - shift, 0, tiles - 1)
        return remote(
            psend.at[j, pl.ds(begin, end - begin)],
            precv.at[at, j, pl.ds(begin, end - begin)],
            p_send.at[at, j],
            p_recv.at[at, j],
            (m, to),
        )

    def pull(j, carry):
        depth = pl.ds(pl.multiple_of(j * width, width), width)
        product = lax.dot_general(
            edges[...], cmap[depth, :], (((1,), (1,)), ((), ())), preferred_element_type=F32
        ).reshape(ext, mem, width)
        pown[j] = product
        psend[j] = product.astype(BF16)
        for at, shift in enumerate(shifts):

            @pl.when(has_target(-shift))
            def _():
                pulled_copy(at, j).start()

        return carry

    lax.fori_loop(0, chunks, pull, 0)

    def second_forward(j, square):
        for at, shift in enumerate(shifts):

            @pl.when(has_target(shift))
            def _():
                pulled_copy(at, j).wait_recv()

        pieces = []
        for lane in range(width // LANES):
            cols = pl.ds(lane * LANES, LANES)
            lowest = -rows - KSM
            pulled = [None] * (rows + 2 * (rows + KSM))

            def put(row, value):
                at = row - lowest
                if 0 <= at < len(pulled):
                    pulled[at] = value if pulled[at] is None else pulled[at] + value

            for e in range(ext):
                value = pown[j, e, :, cols]
                if e == 0:
                    value = value * low1
                if e == ext - 1:
                    value = value * high1
                put(e - 1, value)
            for at, shift in enumerate(shifts):
                begin, end = spans[shift]
                for e in range(begin, end):
                    row = shift * rows + e - 1
                    value = precv[at, j, e, :, cols].astype(F32)
                    mask = mask_of(row)
                    put(row, value if mask is None else value * mask)
            smooth = sweep(pulled, lowest, mask_of)
            slope = [a + b for a, b in zip(smooth, extended_weights(j, lane))]
            for r in range(rows):
                own = slope[rows + r]
                grad[j, r, :, cols] = own
                square = square + own * own
            pieces.append(sweep(slope, -rows, mask_of))
        map_chunk(j, smooth_to_lhs(pieces))
        return square

    square = lax.fori_loop(0, chunks, second_forward, jnp.zeros((mem, LANES), F32))
    total_square = jnp.sum(jnp.sum(square, axis=0, keepdims=True), axis=1, keepdims=True)
    hsend[1, scalar_row : scalar_row + 1, :] = jnp.broadcast_to(total_square, (1, slots))
    observe(1, None)

    state = gathered(1)
    curve = jnp.zeros((1, slots), F32)
    for k in range(members):
        here = state[k : k + 1]
        curve = curve + fields[k][3:4] * here * here
    curve = jnp.sum(curve, axis=1, keepdims=True)
    norm = state[scalar_row : scalar_row + 1, 0:LANES]
    ids = lax.broadcasted_iota(jnp.int32, (8, LANES), 0)
    ssend[...] = jnp.where(
        ids == 0, jnp.broadcast_to(norm, (8, LANES)), jnp.broadcast_to(curve, (8, LANES))
    )

    def scalar_copy(d):
        to = lax.rem(t + d, tiles)
        return remote(ssend, srecv.at[t], s_send.at[d], s_recv.at[d], (m, to))

    for d in range(1, tiles):
        scalar_copy(d).start()
    srecv[t] = ssend[...]
    for which in range(2):
        frecv[which, m] = part[which, m]
        for d in range(1, members):
            part_copy(which, d).wait_recv()
    increment = frecv[0, 0]
    image = frecv[1, 0]
    for k in range(1, members):
        increment = increment + frecv[0, k]
        image = image + frecv[1, k]
    for d in range(1, tiles):
        scalar_copy(d).wait_recv()
    sums = srecv[0]
    for k in range(1, tiles):
        sums = sums + srecv[k]
    norm = sums[0:1, 0:1]
    step = norm / (norm + sums[1:2, 0:1])
    outi_ref[...] = increment - step * image
    step_row = jnp.broadcast_to(step, (mem, width))

    def write(j, carry):
        for r in range(rows):
            outw_ref[j, r] = w_ref[j, r] - step_row * grad[j, r]
        return carry

    lax.fori_loop(0, chunks, write, 0)

    for d in range(1, tiles):
        first_obs(d).wait_send()
        scalar_copy(d).wait_send()
    for d in range(1, members):
        second_obs(d).wait_send()
        for which in range(2):
            h_copy(which, d).wait_send()
            part_copy(which, d).wait_send()

    def drain(j, carry):
        for side in range(2):

            @pl.when(has_target(1 - 2 * side))
            def _():
                halo_copy(side, j).wait_send()

        for at, shift in enumerate(shifts):

            @pl.when(has_target(-shift))
            def _():
                pulled_copy(at, j).wait_send()

        return carry

    lax.fori_loop(0, chunks, drain, 0)


def shards(
    perturb,
    weights,
    column_map,
    background,
    stencil_index,
    row_fraction,
    column_fraction,
    block_lengths,
    obs_value,
    obs_error,
    instrument_gain,
):
    members = lax.axis_size("member")
    tiles = lax.axis_size("tile")
    fine_rows, region = background.shape
    mem, rows, coarse_cols = weights.shape
    fine_cols = column_map.shape[1]
    _, batches, owners, cap = stencil_index.shape
    slots = batches * cap
    chunks = coarse_cols // BLOCK
    ext = rows + 2
    assert rows == KSM + 1 and owners == members and members * cap <= LANES

    def by_owner(values):
        return jnp.transpose(values[0], (1, 0, 2)).reshape(owners, slots)

    index = by_owner(stencil_index)
    live = lax.broadcasted_iota(jnp.int32, (owners, batches, cap), 2) < block_lengths[0].T[..., None]
    rows_of = [
        (index // region).astype(F32),
        (index % region).astype(F32),
        by_owner(row_fraction),
        by_owner(column_fraction),
        live.astype(F32).reshape(owners, slots),
    ]
    obs = jnp.pad(jnp.stack(rows_of, axis=1), ((0, 0), (0, 3), (0, 0)))

    def by_tile(values):
        arranged = jnp.transpose(values.reshape(members, tiles, cap), (1, 0, 2))
        return jnp.pad(
            arranged.reshape(tiles, members * cap), ((0, 0), (0, LANES - members * cap))
        )

    pay = jnp.stack(
        [
            by_tile(obs_value[0]),
            by_tile(obs_error[0]),
            jnp.broadcast_to(instrument_gain[0], (tiles, LANES)),
        ],
        axis=1,
    )
    pay = jnp.pad(pay, ((0, 0), (0, 5), (0, 0)))
    w_rows = jnp.transpose(weights.reshape(mem, rows, chunks, BLOCK), (2, 1, 0, 3))
    per_rows = jnp.transpose(perturb, (1, 0, 2))

    lines = (members + 7) // 8 * 8 + 8
    vmem = pl.BlockSpec(memory_space=pltpu.VMEM)
    hbm = pl.BlockSpec(memory_space=pl.ANY)
    dma = pltpu.SemaphoreType.DMA
    out_w, increment = pl.pallas_call(
        functools.partial(kernel, members, tiles),
        out_shape=(
            jax.ShapeDtypeStruct(w_rows.shape, F32),
            jax.ShapeDtypeStruct(background.shape, F32),
        ),
        in_specs=[vmem, vmem, vmem, vmem, hbm, hbm],
        out_specs=(vmem, vmem),
        scratch_shapes=[
            pltpu.VMEM(column_map.shape, BF16),
            pltpu.VMEM(per_rows.shape, BF16),
            pltpu.VMEM((members, region, 2 * slots), BF16),
            pltpu.VMEM((members, fine_rows, slots), F32),
            pltpu.VMEM((members, 8, slots), F32),
            pltpu.VMEM((members, tiles, 8, LANES), F32),
            pltpu.VMEM(w_rows.shape, BF16),
            pltpu.VMEM((2,) + w_rows.shape, BF16),
            pltpu.VMEM((ext * mem, fine_cols), F32),
            pltpu.VMEM((fine_rows, fine_cols), F32),
            pltpu.VMEM((2, members, fine_rows, region), F32),
            pltpu.VMEM((2, members, fine_rows, region), F32),
            pltpu.VMEM((2, lines, slots), F32),
            pltpu.VMEM((2, members, lines, slots), F32),
            pltpu.VMEM((8, LANES), F32),
            pltpu.VMEM((tiles, 8, LANES), F32),
            pltpu.VMEM((fine_rows, fine_cols), F32),
            pltpu.VMEM((ext * mem, fine_cols), BF16),
            pltpu.VMEM((chunks, ext, mem, BLOCK), F32),
            pltpu.VMEM((chunks, ext, mem, BLOCK), BF16),
            pltpu.VMEM((4, chunks, ext, mem, BLOCK), BF16),
            pltpu.VMEM(w_rows.shape, F32),
            dma((2,)),
            dma((tiles,)),
            dma((tiles,)),
            dma((members,)),
            dma((members,)),
            dma((2, chunks)),
            dma((2, chunks)),
            dma((2, members)),
            dma((2, members)),
            dma((2, members)),
            dma((2, members)),
            dma((4, chunks)),
            dma((4, chunks)),
            dma((tiles,)),
            dma((tiles,)),
        ],
        compiler_params=pltpu.CompilerParams(
            collective_id=0, has_side_effects=True, vmem_limit_bytes=50 * 2**20
        ),
    )(pay, w_rows, obs, background, column_map, per_rows)
    analysis = jnp.transpose(out_w, (2, 1, 0, 3)).reshape(weights.shape)
    return analysis, increment


def solution(mesh):
    placed = (
        P("member", "tile", None),
        P("member", "tile", None),
        P(),
        P("tile", "member"),
        P("tile", None, None, None),
        P("tile", None, None, None),
        P("tile", None, None, None),
        P("tile", None, None),
        P(("member", "tile"), None, None),
        P(("member", "tile"), None, None),
        P(("member", "tile")),
    )
    return jax.shard_map(
        shards,
        mesh=mesh,
        in_specs=placed,
        out_specs=(P("member", "tile", None), P("tile", "member")),
        check_vma=False,
    )
```

time: 214 us -> 55.2 us (0.26)
  waiting for transfers between devices: 86.7 us -> 0 us
  Pallas kernels: 0 us -> 43.4 us
  blocking collectives: 39.6 us -> 0 us
  starting transfers between devices: 33.7 us -> 0 us
  between operations: 17.1 us -> 1.46 us
  matrix products: 14.1 us -> 0 us
  other arithmetic: 11.8 us -> 1.56 us
  local copies, waits for them, and re-layouts: 10.5 us -> 8.21 us
    pallas_call x0 -> x1, Pallas kernels: none -> 43.4 us  [shards(): pl.pallas_call(functools.partial(kernel, members, tiles), out_shape=(jax....]
    psum x1 -> x0, blocking collectives: 39.6 us -> none  [global_sum(): return lax.psum(values, ('member', 'tile'))]
    reduce_scatter x2 -> x0, waiting for transfers between devices: 39 us -> none  [forward(): lax.psum_scatter(member_term, 'member', scatter_dimension=1, tiled=True)]
    ppermute x8 -> x0, waiting for transfers between devices: 34.2 us -> none  [the longest x4 25.8 us: padded(): lax.ppermute(lax.slice_in_dim(block, block.shape[dim] - width, None, axis...]
    ppermute x8 -> x0, starting transfers between devices: 22.4 us -> none  [the longest x4 17.3 us: padded(): lax.ppermute(lax.slice_in_dim(block, block.shape[dim] - width, None, axis...]
    dot_general x6 -> x0, matrix products: 14.1 us -> none  [the longest x2 5.29 us: forward(): jnp.dot(extended.astype(jnp.bfloat16).reshape(-1, coarse_cols), column_ma...]
    all_to_all x3 -> x0, waiting for transfers between devices: 13.4 us -> none  [the longest x1 7.2 us: shards(): lax.all_to_all(fan_out(residual), ('member', 'tile'), split_axis=0, conca...]
    all_to_all x3 -> x0, starting transfers between devices: 11 us -> none  [the longest x1 4.58 us: shards(): lax.all_to_all(obs_state, ('member', 'tile'), split_axis=0, concat_axis=0...]
  transfers between devices with their start and end apart: 13 -> 0, of which waited for: 11 -> 0; matrix products, arithmetic and copies ran while one was open for 6% -> 0% of each run, Pallas kernels for 0% -> 0%
where the time goes in v1:
time: 55.2 us; the launch traced here: 54.6 us
  Pallas kernels  43.4 us (79%)
  local copies, waits for them, and re-layouts  8.21 us (15%)
  other arithmetic  1.56 us (3%)
  between operations  1.46 us (3%)
    pallas_call x1, Pallas kernels, shards(): pl.pallas_call(functools.partial(kernel, members, tiles), out_shape=(jax....  43.4 us
    unnamed x10, local copies, waits for them, and re-layouts  2.51 us
    another operation x4, local copies, waits for them, and re-layouts, by_tile(): arranged = jnp.transpose(values.reshape(members, tiles, cap), (1, 0, 2))  1.7 us
    transpose x2, local copies, waits for them, and re-layouts, by_owner(): return jnp.transpose(values[0], (1, 0, 2)).reshape(owners, slots)  1.59 us

profile of v1, /device:TPU:0, one launch (start us, length us, event | category | flops | bytes accessed | tf_op | source)
XLA Modules:
  0.0 54.6 jit_solution(2323169058206082888)
XLA Ops:
  1.3 0.1 pad.21.clone
  1.4 0.7 %fusion = pred[4,32,8]{1,2,0:T(8,128)(4,1)S(1)} fusion(s32[1,32,4,8]{1,3,2,0:T(8,128)} %param.15), kind=kLoop, calls=%fused_computation.6 | loop fusion | flops 2048 | bytes 5120 | tf_op jit(solution)/shard_map/jit(floor_divide)/ne | solution.py:544
  2.1 0.1 copy.47
  2.2 0.1 ne.63
  2.3 0.8 %reshape_squeeze.6 = f32[4,8,8]{1,0,2:T(4,128)S(1)} reshape(f32[1,32,8]{1,2,0:T(8,128)} %param.19) | data formatting | bytes 2048 | tf_op jit(solution)/shard_map/reshape;squeeze | solution.py:553
  3.1 0.1 copy.43
  3.2 0.1 reshape.134
  3.3 0.8 %reshape_squeeze.7 = f32[4,8,8]{1,0,2:T(4,128)S(1)} reshape(f32[1,32,8]{1,2,0:T(8,128)} %param.20) | data formatting | bytes 2048 | tf_op jit(solution)/shard_map/reshape;squeeze | solution.py:553
  4.1 0.1 copy.44
  4.1 0.1 reshape.135
  4.2 0.1 maximum_maximum_fusion
  4.3 0.1 iota.12
  4.4 0.7 %remainder_bitcast_fusion = (s32[4,32,8]{1,2,0:T(8,128)S(1)}, s32[4,32,8]{1,2,0:T(8,128)S(1)}) fusion(s32[1,32,4,8]{1,3,2,0:T(8,128)} %param.15), kind=kLoop, calls=%fused_computation.4 | loop fusion | flops 2048 | bytes 12288 | tf_op jit(solution)/shard_map/jit(floor_divide)/rem | solution.py:544
  5.2 0.0 copy-start.1
  5.2 0.1 copy.48
  5.2 0.1 rem.40
  5.3 0.1 copy.51
  5.4 0.1 div.26
  5.6 0.8 %copy.57 = f32[4,32,8]{2,1,0:T(8,128)S(1)} copy(f32[4,32,8]{1,2,0:T(8,128)} %bitcast.42) | data formatting | bytes 8192 | tf_op jit(solution)/shard_map/transpose | solution.py:539
  6.4 0.1 stack_reshape.9
  6.5 0.8 %copy.58 = f32[4,32,8]{2,1,0:T(8,128)S(1)} copy(f32[4,32,8]{1,2,0:T(8,128)} %bitcast.43) | data formatting | bytes 8192 | tf_op jit(solution)/shard_map/transpose | solution.py:539
  7.3 0.1 stack_reshape.10
  7.4 0.8 %lt.24 = s32[4,32,8]{2,1,0:T(8,128)S(1)} broadcast(s32[4,32]{1,0:T(4,128)} %bitcast.46), dimensions={0,1} | broadcast | bytes 4608 | tf_op jit(solution)/shard_map/lt | solution.py:542
  8.1 0.1 lt.27
  8.3 0.2 reshape.138
  8.5 0.2 copy.73
  8.7 0.7 %copy.72 = bf16[16,16,2560]{2,0,1:T(8,128)(2,1)S(1)} copy(bf16[16,16,2560]{2,1,0:T(8,128)(2,1)S(1)} %copy-done.1) | data formatting | bytes 2621440 | tf_op args[0]
  9.4 0.0 copy-done
  9.5 43.4 %shard_map.122 = (f32[5,4,16,256]{3,2,1,0:T(8,128)S(1)}, f32[16,640]{1,0:T(8,128)S(1)}) custom-call(f32[8,8,128]{2,1,0:T(8,128)S(1)} %pad.17.pay_ref, f32[5,4,16,256]{3,2,1,0:T(8,128)S(1)} %bitcast.38, f32[4,8,256]{2,1,0:T(8,128)S(1)} %pad.18.obs_ref, f32[16,640]{1,0:T(8,128)S(1)} %copy-done, bf16[1280,2560]{1,0:T(8,128)(2,1)} %map_hbm.1, ...), custom_call_target="tpu_custom_call" | custom-call | tf_op jit(solution)/shard_map/pallas_call | solution.py:574
  52.9 0.2 copy.68
  53.1 0.9 %reshape.139 = f32[16,4,1280]{2,1,0:T(4,128)} reshape(f32[16,4,5,256]{3,2,1,0:T(8,128)S(1)} %copy.68) | data formatting | bytes 655360
  54.0 0.6 %copy.76 = f32[16,640]{1,0:T(8,128)} copy(f32[16,640]{1,0:T(8,128)S(1)} %get-tuple-element.17) | data formatting | bytes 81920
  (12 shorter events, 0.1 us)
Async XLA Ops:
  0.6 7.7 %copy-start.2 = (f32[16,4,1280]{2,1,0:T(4,128)S(1)}, f32[16,4,1280]{2,1,0:T(4,128)}, u32[]{:S(2)}) copy-start(f32[16,4,1280]{2,1,0:T(4,128)} %param.12) | copy-start | bytes 983044
  5.2 3.5 %copy-start.1 = (bf16[16,16,2560]{2,1,0:T(8,128)(2,1)S(1)}, bf16[16,16,2560]{2,1,0:T(8,128)(2,1)}, u32[]{:S(2)}) copy-start(bf16[16,16,2560]{2,1,0:T(8,128)(2,1)} %param.11) | copy-start | bytes 3932164
  8.7 0.8 %copy-start = (f32[16,640]{1,0:T(8,128)S(1)}, f32[16,640]{1,0:T(8,128)}, u32[]{:S(2)}) copy-start(f32[16,640]{1,0:T(8,128)} %bg_ref.1) | copy-start | bytes 122884

commit v2 on v1

--- a/solution.py
+++ b/solution.py
@@ -51,7 +51,7 @@
     per,
     hot,
     rowf,
-    fields,
+    info,
     obsin,
     wsend,
     halo,
@@ -87,10 +87,12 @@
 ):
     m = lax.axis_index("member")
     t = lax.axis_index("tile")
-    chunks, rows, mem, width = w_ref.shape
+    rows, mem, coarse_cols = w_ref.shape
+    width = BLOCK
+    chunks = coarse_cols // width
     region = bg_ref.shape[1]
     fine_rows = bg_ref.shape[0]
-    slots = obs_ref.shape[2]
+    slots = rowf.shape[2]
     fine_cols = cmap.shape[1]
     ext = rows + 2
     cap = slots // (members * tiles)
@@ -111,7 +113,8 @@
             barrier, inc=1, device_id=(m, lax.rem(t + d, tiles)), device_id_type=MESH
         )
 
-    wsend[...] = w_ref[...].astype(BF16)
+    for j in range(chunks):
+        wsend[j] = w_ref[:, :, j * width : (j + 1) * width].astype(BF16)
     obsin[m, t] = pay_ref[t]
     pl.semaphore_wait(barrier, members + tiles - 2)
 
@@ -166,9 +169,33 @@
 
     hsend[...] = jnp.zeros(hsend.shape, hsend.dtype)
 
-    def prepare(k, carry):
-        info = obs_ref[k]
-        row_pos, col_pos, row_frac = info[0:1], info[1:2], info[2:3]
+    owner_ids = lax.broadcasted_iota(jnp.int32, (members * tiles, 8, slots), 0)
+    lane_ids = lax.broadcasted_iota(jnp.int32, (members * tiles, 8, slots), 2)
+    chosen = lane_ids // cap == owner_ids
+    source = lax.broadcasted_iota(jnp.int32, (LANES, slots), 0)
+    target = lax.broadcasted_iota(jnp.int32, (LANES, slots), 1)
+
+    def arranged(listed, field):
+        pick = jnp.where(source == field * cap + target % cap, 1.0, 0.0).astype(F32)
+        wide = jnp.dot(
+            listed.reshape(members * tiles * 8, LANES),
+            pick,
+            precision=lax.Precision.HIGHEST,
+            preferred_element_type=F32,
+        ).reshape(members * tiles, 8, slots)
+        return jnp.sum(jnp.where(chosen, wide, 0.0), axis=0)
+
+    listed = obs_ref[...]
+    index = (arranged(listed, 0) + 0.5).astype(jnp.int32)
+    info[0] = (index // region).astype(F32)
+    info[1] = (index % region).astype(F32)
+    info[2] = arranged(listed, 1)
+    info[3] = arranged(listed, 2)
+    slot_ids = lax.broadcasted_iota(jnp.int32, (8, slots), 1) % cap
+    info[4] = jnp.where(slot_ids.astype(F32) < arranged(listed, 3), 1.0, 0.0)
+
+    for k in range(members):
+        row_pos, col_pos, row_frac = (info[f, k : k + 1] for f in range(3))
         col_ids = lax.broadcasted_iota(jnp.int32, (region, slots), 0).astype(F32)
         hot[k, :, 0:slots] = jnp.where(col_ids == col_pos, 1.0, 0.0).astype(BF16)
         hot[k, :, slots : 2 * slots] = jnp.where(col_ids == col_pos + 1.0, 1.0, 0.0).astype(BF16)
@@ -176,9 +203,6 @@
         rowf[k] = jnp.where(row_ids == row_pos, 1.0 - row_frac, 0.0) + jnp.where(
             row_ids == row_pos + 1.0, row_frac, 0.0
         )
-        return carry
-
-    lax.fori_loop(0, members, prepare, 0)
 
     for d in range(1, tiles):
         first_obs(d).wait_recv()
@@ -203,9 +227,10 @@
 
     def extended_weights(j, at):
         cols = pl.ds(at * LANES, LANES)
+        whole = pl.ds(pl.multiple_of(j * width + at * LANES, LANES), LANES)
         return (
             [halo[0, j, r, :, cols].astype(F32) for r in range(rows)]
-            + [w_ref[j, r, :, cols] for r in range(rows)]
+            + [w_ref[r, :, whole] for r in range(rows)]
             + [halo[1, j, r, :, cols].astype(F32) for r in range(rows)]
         )
 
@@ -288,7 +313,7 @@
                 field = field + bg_ref[...] * jnp.where(m == k, 1.0, 0.0).astype(F32)
             found = jnp.dot(split_rows(field), hot[k], preferred_element_type=F32)
             found = found[:fine_rows] + found[fine_rows:]
-            col_frac = obs_ref[k][3:4]
+            col_frac = info[3, k : k + 1]
             along = (1.0 - col_frac) * found[:, :slots] + col_frac * found[:, slots:]
             hsend[which, k : k + 1, :] = jnp.sum(along * rowf[k], axis=0, keepdims=True)
         for d in range(1, members):
@@ -309,30 +334,20 @@
 
     for d in range(1, members):
         second_obs(d).wait_recv()
-    listed = obsin[...].reshape(members * tiles * 8, LANES)
-    owner_ids = lax.broadcasted_iota(jnp.int32, (members * tiles, 8, slots), 0)
-    lane_ids = lax.broadcasted_iota(jnp.int32, (members * tiles, 8, slots), 2)
-    chosen = lane_ids // cap == owner_ids
-    source = lax.broadcasted_iota(jnp.int32, (LANES, slots), 0)
-    target = lax.broadcasted_iota(jnp.int32, (LANES, slots), 1)
+    listed = obsin[...].reshape(members * tiles, 8, LANES)
+    value, error, gain = (arranged(listed, f) for f in range(3))
+    precision = 1.0 / (error * error)
+
+    state = gathered(0)
+
+    here = state[0:8]
+    bounded = jnp.tanh(here)
+    slope = 1.0 + gain * (1.0 - bounded * bounded)
+    info[5] = slope * (here + gain * bounded - value) * precision * info[4]
+    info[6] = slope * slope * precision * info[4]
+
     for k in range(members):
-        pick = jnp.where(source == k * cap + target % cap, 1.0, 0.0).astype(F32)
-        wide = jnp.dot(listed, pick, precision=lax.Precision.HIGHEST, preferred_element_type=F32)
-        wide = wide.reshape(members * tiles, 8, slots)
-        fields[k] = jnp.sum(jnp.where(chosen, wide, 0.0), axis=0)
-
-    state = gathered(0)
-
-    for k in range(members):
-        value, error, gain = fields[k][0:1], fields[k][1:2], fields[k][2:3]
-        here = state[k : k + 1]
-        bounded = jnp.tanh(here)
-        slope = 1.0 + gain * (1.0 - bounded * bounded)
-        precision = 1.0 / (error * error)
-        live = obs_ref[k][4:5]
-        residual = slope * (here + gain * bounded - value) * precision * live
-        fields[k, 3:4] = slope * slope * precision * live
-        col_frac = obs_ref[k][3:4]
+        residual, col_frac = info[5, k : k + 1], info[3, k : k + 1]
         weighted = rowf[k] * residual
         both = jnp.concatenate([weighted * (1.0 - col_frac), weighted * col_frac], axis=1)
         found = lax.dot_general(
@@ -443,7 +458,7 @@
     curve = jnp.zeros((1, slots), F32)
     for k in range(members):
         here = state[k : k + 1]
-        curve = curve + fields[k][3:4] * here * here
+        curve = curve + info[6, k : k + 1] * here * here
     curve = jnp.sum(curve, axis=1, keepdims=True)
     norm = state[scalar_row : scalar_row + 1, 0:LANES]
     ids = lax.broadcasted_iota(jnp.int32, (8, LANES), 0)
@@ -479,7 +494,8 @@
 
     def write(j, carry):
         for r in range(rows):
-            outw_ref[j, r] = w_ref[j, r] - step_row * grad[j, r]
+            cols = pl.ds(pl.multiple_of(j * width, width), width)
+            outw_ref[r, :, cols] = w_ref[r, :, cols] - step_row * grad[j, r]
         return carry
 
     lax.fori_loop(0, chunks, write, 0)
@@ -533,38 +549,22 @@
     slots = batches * cap
     chunks = coarse_cols // BLOCK
     ext = rows + 2
-    assert rows == KSM + 1 and owners == members and members * cap <= LANES
-
-    def by_owner(values):
-        return jnp.transpose(values[0], (1, 0, 2)).reshape(owners, slots)
-
-    index = by_owner(stencil_index)
-    live = lax.broadcasted_iota(jnp.int32, (owners, batches, cap), 2) < block_lengths[0].T[..., None]
-    rows_of = [
-        (index // region).astype(F32),
-        (index % region).astype(F32),
-        by_owner(row_fraction),
-        by_owner(column_fraction),
-        live.astype(F32).reshape(owners, slots),
-    ]
-    obs = jnp.pad(jnp.stack(rows_of, axis=1), ((0, 0), (0, 3), (0, 0)))
-
-    def by_tile(values):
-        arranged = jnp.transpose(values.reshape(members, tiles, cap), (1, 0, 2))
+    assert rows == KSM + 1 and owners == members and members <= 8 and 4 * cap <= LANES
+
+    def rows_of(parts):
+        parts = jnp.concatenate(parts, axis=-1)
         return jnp.pad(
-            arranged.reshape(tiles, members * cap), ((0, 0), (0, LANES - members * cap))
-        )
-
-    pay = jnp.stack(
-        [
-            by_tile(obs_value[0]),
-            by_tile(obs_error[0]),
-            jnp.broadcast_to(instrument_gain[0], (tiles, LANES)),
-        ],
-        axis=1,
+            parts, ((0, 0), (0, 8 - parts.shape[1]), (0, LANES - parts.shape[2]))
+        )
+
+    lengths = jnp.broadcast_to(block_lengths[0][..., None], stencil_index.shape[1:])
+    obs = rows_of(
+        [stencil_index[0].astype(F32), row_fraction[0], column_fraction[0], lengths.astype(F32)]
     )
-    pay = jnp.pad(pay, ((0, 0), (0, 5), (0, 0)))
-    w_rows = jnp.transpose(weights.reshape(mem, rows, chunks, BLOCK), (2, 1, 0, 3))
+    gain = jnp.broadcast_to(instrument_gain, obs_value.shape[1:])
+    batch = jnp.concatenate([obs_value[0], obs_error[0], gain], axis=-1)
+    pay = rows_of([jnp.transpose(batch.reshape(members, tiles, 3 * cap), (1, 0, 2))])
+    w_rows = jnp.transpose(weights, (1, 0, 2))
     per_rows = jnp.transpose(perturb, (1, 0, 2))
 
     lines = (members + 7) // 8 * 8 + 8
@@ -584,10 +584,10 @@
             pltpu.VMEM(per_rows.shape, BF16),
             pltpu.VMEM((members, region, 2 * slots), BF16),
             pltpu.VMEM((members, fine_rows, slots), F32),
-            pltpu.VMEM((members, 8, slots), F32),
+            pltpu.VMEM((7, 8, slots), F32),
             pltpu.VMEM((members, tiles, 8, LANES), F32),
-            pltpu.VMEM(w_rows.shape, BF16),
-            pltpu.VMEM((2,) + w_rows.shape, BF16),
+            pltpu.VMEM((chunks, rows, mem, BLOCK), BF16),
+            pltpu.VMEM((2, chunks, rows, mem, BLOCK), BF16),
             pltpu.VMEM((ext * mem, fine_cols), F32),
             pltpu.VMEM((fine_rows, fine_cols), F32),
             pltpu.VMEM((2, members, fine_rows, region), F32),
@@ -601,7 +601,7 @@
             pltpu.VMEM((chunks, ext, mem, BLOCK), F32),
             pltpu.VMEM((chunks, ext, mem, BLOCK), BF16),
             pltpu.VMEM((4, chunks, ext, mem, BLOCK), BF16),
-            pltpu.VMEM(w_rows.shape, F32),
+            pltpu.VMEM((chunks, rows, mem, BLOCK), F32),
             dma((2,)),
             dma((tiles,)),
             dma((tiles,)),
@@ -622,8 +622,7 @@
             collective_id=0, has_side_effects=True, vmem_limit_bytes=50 * 2**20
         ),
     )(pay, w_rows, obs, background, column_map, per_rows)
-    analysis = jnp.transpose(out_w, (2, 1, 0, 3)).reshape(weights.shape)
-    return analysis, increment
+    return jnp.transpose(out_w, (1, 0, 2)), increment
 
 
 def solution(mesh):

time: 55.2 us -> 54.2 us (0.982)
  local copies, waits for them, and re-layouts: 8.21 us -> 7.03 us
    unnamed x10 -> x11, local copies, waits for them, and re-layouts: 2.51 us -> 5.06 us
    another operation x8 -> x0, local copies, waits for them, and re-layouts: 2.03 us -> none  [the longest x4 1.7 us: by_tile(): arranged = jnp.transpose(values.reshape(members, tiles, cap), (1, 0, 2))]
    concatenate x0 -> x5, local copies, waits for them, and re-layouts: none -> 1.77 us  [shards(): batch = jnp.concatenate([obs_value[0], obs_error[0], gain], axis=-1)]
    transpose x2 -> x0, local copies, waits for them, and re-layouts: 1.59 us -> none  [by_owner(): return jnp.transpose(values[0], (1, 0, 2)).reshape(owners, slots)]
    convert_element_type x2, other arithmetic: 0.03 us -> 1.4 us  [the longest x1 0.72 us: shards(): stencil_index[0].astype(F32)]
    lt x2 -> x0, local copies, waits for them, and re-layouts: 0.86 us -> none  [shards(): lax.broadcasted_iota(jnp.int32, (owners, batches, cap), 2)]
    rem x1 -> x0, other arithmetic: 0.73 us -> none  [shards(): index // region]
    ne x1 -> x0, other arithmetic: 0.72 us -> none  [shards(): index // region]
where the time goes in v2:
time: 54.2 us; the launch traced here: 53.7 us
  Pallas kernels  43.5 us (80%)
  local copies, waits for them, and re-layouts  7.03 us (13%)
  other arithmetic  1.66 us (3%)
  between operations  1.47 us (3%)
    pallas_call x1, Pallas kernels, shards(): pl.pallas_call(functools.partial(kernel, members, tiles), out_shape=(jax....  43.5 us
    unnamed x11, local copies, waits for them, and re-layouts  5.06 us
    concatenate x5, local copies, waits for them, and re-layouts, shards(): batch = jnp.concatenate([obs_value[0], obs_error[0], gain], axis=-1)  1.77 us

profile of v2, /device:TPU:0, one launch (start us, length us, event | category | flops | bytes accessed | tf_op | source)
XLA Modules:
  0.0 53.7 jit_solution(10439700171705814856)
XLA Ops:
  0.6 0.0 copy-start.1
  1.4 0.1 pad.16.clone
  1.5 0.7 %convert_bitcast_fusion = f32[32,4]{0,1:T(4,128)S(1)} fusion(s32[1,32,4]{1,2,0:T(4,128)} %param.18), kind=kLoop, calls=%fused_computation.8 | loop fusion | flops 128 | bytes 1024 | tf_op jit(solution)/shard_map/convert_element_type | solution.py:562
  2.2 0.1 copy.26
  2.2 0.7 %convert_element_type.21 = f32[1,32,4,8]{1,3,2,0:T(8,128)S(1)} convert(s32[1,32,4,8]{1,3,2,0:T(8,128)} %param.15) | non-fusion elementwise | flops 1024 | bytes 8192 | tf_op jit(solution)/shard_map/convert_element_type | solution.py:562
  3.0 0.8 %concatenate.11 = f32[4,8,8]{1,0,2:T(4,128)S(1)} reshape(f32[1,32,8]{1,2,0:T(8,128)} %param.19) | data formatting | bytes 2048 | tf_op jit(solution)/shard_map/concatenate | solution.py:565
  3.7 0.1 copy.20
  3.8 0.8 %concatenate.12 = f32[4,8,8]{1,0,2:T(4,128)S(1)} reshape(f32[1,32,8]{1,2,0:T(8,128)} %param.20) | data formatting | bytes 2048 | tf_op jit(solution)/shard_map/concatenate | solution.py:565
  4.6 0.1 copy.21
  4.7 0.1 maximum_bitcast_fusion
  4.8 0.1 copy.29
  4.9 0.1 broadcast_in_dim.5
  5.0 0.8 %copy.24 = f32[1,32,4,8]{3,2,1,0:T(4,128)S(1)} copy(f32[1,32,4,8]{1,3,2,0:T(8,128)} %param.16) | data formatting | bytes 8192 | tf_op args[5]
  5.8 0.8 %copy.25 = f32[1,32,4,8]{3,2,1,0:T(4,128)S(1)} copy(f32[1,32,4,8]{1,3,2,0:T(8,128)} %param.17) | data formatting | bytes 8192 | tf_op args[6]
  6.6 0.2 select_maximum_fusion.obs_ref
  6.8 1.0 %copy.33 = f32[16,4,1280]{2,0,1:T(8,128)S(1)} copy(f32[16,4,1280]{2,1,0:T(4,128)} %param.12) | data formatting | bytes 655360 | tf_op args[1]
  7.8 0.0 copy-done.1
  7.8 0.0 copy-start
  7.8 0.7 %copy.32 = bf16[16,16,2560]{2,0,1:T(8,128)(2,1)S(1)} copy(bf16[16,16,2560]{2,1,0:T(8,128)(2,1)S(1)} %copy-done.1) | data formatting | bytes 2621440 | tf_op args[0]
  8.6 0.0 copy-done
  8.6 43.5 %shard_map.125 = (f32[4,16,1280]{2,1,0:T(8,128)S(1)}, f32[16,640]{1,0:T(8,128)S(1)}) custom-call(f32[8,8,128]{2,1,0:T(8,128)S(1)} %pad.8.pay_ref, f32[4,16,1280]{2,1,0:T(8,128)S(1)} %bitcast.21, f32[32,8,128]{2,1,0:T(8,128)S(1)} %select_maximum_fusion.obs_ref, f32[16,640]{1,0:T(8,128)S(1)} %copy-done, bf16[1280,2560]{1,0:T(8,128)(2,1)} %map_hbm.1, ...), custom_call_target="tpu_custom_call" | custom-call | tf_op jit(solution)/shard_map/pallas_call | solution.py:574
  52.1 0.9 %copy.28 = f32[16,4,1280]{2,1,0:T(4,128)} copy(f32[16,4,1280]{2,0,1:T(8,128)S(1)} %bitcast.22) | data formatting | bytes 655360
  53.0 0.6 %copy.36 = f32[16,640]{1,0:T(8,128)} copy(f32[16,640]{1,0:T(8,128)S(1)} %get-tuple-element.13) | data formatting | bytes 81920
  (2 shorter events, 0.0 us)
Async XLA Ops:
  0.6 7.2 %copy-start.1 = (bf16[16,16,2560]{2,1,0:T(8,128)(2,1)S(1)}, bf16[16,16,2560]{2,1,0:T(8,128)(2,1)}, u32[]{:S(2)}) copy-start(bf16[16,16,2560]{2,1,0:T(8,128)(2,1)} %param.11) | copy-start | bytes 3932164
  7.8 0.8 %copy-start = (f32[16,640]{1,0:T(8,128)S(1)}, f32[16,640]{1,0:T(8,128)}, u32[]{:S(2)}) copy-start(f32[16,640]{1,0:T(8,128)} %bg_ref.1) | copy-start | bytes 122884
